TPU v7x, 32 devices: a whole 2x2x4 slice. The times are simulated.
32 devices in a mesh: dp: 4 (over y, x), seq: 4 (over z), expert: 2 (over core).
Axes of the slice: x: 2, y: 2, z: 4, core: 2. Of those that a mesh axis runs over, the one named last changes fastest.
Arguments:
- frames: bfloat16 [8, 512, 1024], P(('dp', 'expert'), 'seq'), may hold values from -6 to 6
- lengths: int32 [8], P(('dp', 'expert')), may hold values from 128 to 512, as said below
- routes: int32 [8, 512, 2], P(('dp', 'expert'), 'seq'), may hold values from 0 to 7, all different within a row; in each aligned block of 128 rows (0 to 127, 128 to 255, ..., all dimensions but the last counted through in order) at most 48 rows name the same one
- norm_conv: float32 [1024], replicated, may hold values from 0.1 to 1.9
- point_in: bfloat16 [1024, 2048], replicated, may hold values from -0.1875 to 0.1875
- depth_kernel: float32 [31, 1024], replicated, may hold values from -1 to 1
- bn_scale: float32 [1024], replicated, may hold values from 0.1 to 1.9
- bn_shift: float32 [1024], replicated, may hold values from -3 to 3
- point_out: bfloat16 [1024, 1024], replicated, may hold values from -0.1875 to 0.1875
- norm_moe: float32 [1024], replicated, may hold values from 0.1 to 1.9
- router: bfloat16 [1024, 8], replicated, may hold values from -0.1875 to 0.1875
- gate_weight: bfloat16 [8, 1024, 4096], P(('seq', 'expert'), None, 'dp'), may hold values from -0.1875 to 0.1875
- up_weight: bfloat16 [8, 1024, 4096], P(('seq', 'expert'), None, 'dp'), may hold values from -0.1875 to 0.1875
- down_weight: bfloat16 [8, 1024, 4096], P(('seq', 'expert'), None, 'dp'), may hold values from -0.09375 to 0.09375
Outputs:
- layer_out: bfloat16 [8, 512, 1024], P(('dp', 'expert'), 'seq')
Inputs may be any that keep to these rules, and one draw needn't show every extreme that they name: `lengths`: each utterance has between 128 and 512 valid frames; some utterance has all 512, some only 128. `routes`: the two experts of a frame differ. Among the 128 frames of one device (aligned blocks of frames of one utterance), no expert is named more than 48 times, and in some blocks one expert is named exactly 48 times. Padded frames are routed too.
All inputs are finite; a program needn't handle non-finite values.
Results may differ from a plain program's by a relative error of at most 0.0085.
Values may be sent and summed in bfloat16 or wider, within the bound.
A program may use at most 128 MiB of HBM per device.

v0:
```python
import jax
import jax.numpy as jnp
from jax import lax
from jax.sharding import PartitionSpec as P


def padded_2(x, sides, width):
    for axis, dim in sides:
        size, length = (lax.axis_size(axis), x.shape[dim])
        up = [(i, (i + 1) % size) for i in range(size - 1)]
        down = [(j, i) for i, j in up]
        last = lax.slice_in_dim(x, length - width, length, axis=dim)
        initial = lax.slice_in_dim(x, 0, width, axis=dim)
        before = lax.ppermute(last, axis, up)
        after = lax.ppermute(initial, axis, down)
        x = jnp.concatenate([before, x, after], axis=dim)
    return x


def layer_norm(values, gain):
    values = values.astype(jnp.float32)
    center = values - jnp.mean(values, axis=-1, keepdims=True)
    spread = jnp.mean(center * center, axis=-1, keepdims=True)
    return center * lax.rsqrt(spread + 1e-05) * gain


def local(
    frames,
    lengths,
    routes,
    norm_conv,
    point_in,
    depth_kernel,
    bn_scale,
    bn_shift,
    point_out,
    norm_moe,
    router,
    gate_weight,
    up_weight,
    down_weight,
):
    frame_rows = frames[0]
    token_count = frame_rows.shape[0]
    model_width = frame_rows.shape[1]
    position = lax.axis_index("seq") * token_count + jnp.arange(token_count, dtype=jnp.int32)
    frame_mask = (position < lengths[0]).astype(jnp.float32)[:, None]
    conv_in = layer_norm(frame_rows, norm_conv).astype(jnp.bfloat16)
    lifted = jnp.dot(conv_in, point_in, preferred_element_type=jnp.float32)
    gated = (lifted[:, :model_width] * jax.nn.sigmoid(lifted[:, model_width:]) * frame_mask).astype(
        jnp.bfloat16
    )
    reach = depth_kernel.shape[0] // 2
    padded = padded_2(gated, (("seq", 0),), reach)
    depth = jnp.zeros((token_count, model_width), jnp.float32)
    for offset in range(depth_kernel.shape[0]):
        depth = (
            depth + padded[offset : offset + token_count].astype(jnp.float32) * depth_kernel[offset]
        )
    swished = jax.nn.silu(depth * bn_scale + bn_shift).astype(jnp.bfloat16)
    residual = frame_rows.astype(jnp.float32) + jnp.dot(
        swished, point_out, preferred_element_type=jnp.float32
    )
    moe_in = layer_norm(residual, norm_moe).astype(jnp.bfloat16)
    logits = jnp.dot(moe_in, router, preferred_element_type=jnp.float32)
    seq_count = lax.axis_size("seq")
    expert_count = seq_count * lax.axis_size("expert")
    capacity = 3 * token_count // expert_count
    choice_ids = routes[0]
    expert_ids = jnp.arange(expert_count, dtype=jnp.int32)
    pick_one = (choice_ids[:, 0:1] == expert_ids[None, :]).astype(jnp.int32)
    pick_two = (choice_ids[:, 1:2] == expert_ids[None, :]).astype(jnp.int32)
    logit_one = jnp.sum(logits * pick_one.astype(jnp.float32), axis=1)
    logit_two = jnp.sum(logits * pick_two.astype(jnp.float32), axis=1)
    weight_one = jax.nn.sigmoid(logit_one - logit_two)
    weight_two = jax.nn.sigmoid(logit_two - logit_one)
    both = pick_one + pick_two
    earlier = jnp.cumsum(both, axis=0) - both
    place_one = choice_ids[:, 0] * capacity + jnp.sum(earlier * pick_one, axis=1)
    place_two = choice_ids[:, 1] * capacity + jnp.sum(earlier * pick_two, axis=1)
    slot_ids = jnp.arange(expert_count * capacity, dtype=jnp.int32)
    slot_one = (place_one[:, None] == slot_ids[None, :]).astype(jnp.bfloat16)
    slot_two = (place_two[:, None] == slot_ids[None, :]).astype(jnp.bfloat16)
    outgoing = lax.dot_general(
        slot_one + slot_two, moe_in, (((0,), (0,)), ((), ())), preferred_element_type=jnp.float32
    ).astype(jnp.bfloat16)
    outgoing = outgoing.reshape(expert_count, capacity, model_width)
    gate_local = gate_weight[0]
    up_local = up_weight[0]
    down_local = down_weight[0]
    arrived = lax.all_to_all(outgoing, ("seq", "expert"), split_axis=0, concat_axis=0, tiled=True)
    arrived_shape = arrived.shape
    shard_rows = lax.all_gather(arrived.reshape(-1, arrived_shape[2]), "dp", axis=0, tiled=True)
    gate_part = jnp.dot(shard_rows, gate_local, preferred_element_type=jnp.float32)
    up_part = jnp.dot(shard_rows, up_local, preferred_element_type=jnp.float32)
    hidden = (jax.nn.silu(gate_part) * up_part).astype(jnp.bfloat16)
    summed = lax.psum_scatter(
        lax.dot_general(
            hidden, down_local, (((1,), (1,)), ((), ())), preferred_element_type=jnp.float32
        ).astype(jnp.bfloat16),
        "dp",
        scatter_dimension=0,
        tiled=True,
    )
    served = summed.reshape(arrived_shape)
    returned_rows = lax.all_to_all(
        served, ("seq", "expert"), split_axis=0, concat_axis=0, tiled=True
    )
    returned_rows = returned_rows.reshape(expert_count * capacity, model_width)
    from_one = jnp.dot(slot_one, returned_rows, preferred_element_type=jnp.float32)
    from_two = jnp.dot(slot_two, returned_rows, preferred_element_type=jnp.float32)
    layer_out = (
        residual + weight_one[:, None] * from_one + weight_two[:, None] * from_two
    ) * frame_mask
    return layer_out.astype(jnp.bfloat16)[None]


def solution(mesh):
    return jax.shard_map(
        local,
        mesh=mesh,
        in_specs=(
            P(("dp", "expert"), "seq", None),
            P(("dp", "expert")),
            P(("dp", "expert"), "seq", None),
            P(),
            P(),
            P(),
            P(),
            P(),
            P(),
            P(),
            P(),
            P(("seq", "expert"), None, "dp"),
            P(("seq", "expert"), None, "dp"),
            P(("seq", "expert"), None, "dp"),
        ),
        out_specs=P(("dp", "expert"), "seq", None),
        check_vma=False,
    )
```

profile of v0, /device:TPU:3, one launch (start us, length us, event | category | flops | bytes accessed | tf_op | source)
XLA Modules:
  0.0 192.6 jit_solution(10540216938081758098)
XLA Ops:
  7.3 1.1 convert_reduce_fusion
  8.4 1.2 fusion.13
  9.6 0.0 copy-start.3
  9.6 0.0 copy-start.6
  9.6 0.0 copy-start.2
  9.6 0.0 copy-start.7
  9.7 3.1 %fusion.22 = f32[128,2048]{1,0:T(8,128)S(1)} fusion(bf16[1024,2048]{1,0:T(8,128)(2,1)} %param.18, bf16[1,128,1024]{2,1,0:T(8,128)(2,1)} %param.14, f32[1024]{0:T(1024)} %param.17, f32[128]{0:T(128)S(1)} %add_rsqrt_fusion.1, f32[128]{0:T(128)S(1)} %broadcast_multiply_fusion.1), kind=kOutput, calls=%fused_computation.61 | convolution fusion | flops 537526272 | bytes 5510144 | tf_op jit(solution)/shard_map/dot_general | solution.py:49
  12.8 0.2 fusion.21
  13.0 3.2 %collective-permute-start = (bf16[15,1024]{1,0:T(8,128)(2,1)S(1)}, bf16[15,1024]{1,0:T(8,128)(2,1)S(1)}, u32[]{:S(2)}, u32[]{:S(2)}) collective-permute-start(bf16[15,1024]{1,0:T(8,128)(2,1)S(1)} %get-tuple-element.9), channel_id=1, source_target_pairs={{0,2},{2,4},{4,6},{1,3},{3,5},{5,7},{8,10},{10,12},{12,14},{9,11},... | collective-permute-start | bytes 92168 | tf_op jit(solution)/shard_map/ppermute | solution.py:14
  16.2 1.3 collective-permute-start.1
  17.6 0.1 fusion.74
  17.7 0.1 copy.15
  17.8 0.2 reduce_window_sum.11
  18.1 2.8 %collective-permute-done.1 = bf16[15,1024]{1,0:T(8,128)(2,1)S(1)} collective-permute-done((bf16[15,1024]{1,0:T(8,128)(2,1)S(1)}, bf16[15,1024]{1,0:T(8,128)(2,1)S(1)}, u32[]{:S(2)}, u32[]{:S(2)}) %collective-permute-start.1) | collective-permute-done | bytes 30752 | tf_op jit(solution)/shard_map/ppermute | solution.py:15
  20.9 0.0 copy-start.5
  20.9 5.0 %fusion.76 = (f32[128]{0:T(128)S(1)}, f32[128,1024]{1,0:T(8,128)S(1)}) fusion(bf16[1024,1024]{1,0:T(8,128)(2,1)} %param.22, bf16[128,1024]{1,0:T(8,128)(2,1)S(1)} %fusion.21, bf16[15,1024]{1,0:T(8,128)(2,1)S(1)} %collective-permute-done.1, bf16[15,1024]{1,0:T(8,128)(2,1)S(1)} %collective-permute-done, f32[1024]{0:T(1024)S(1)} %copy-done.7, ...), kind=kOutput, calls=%fused_computation.154 | convolution fusion | flops 293601152 | bytes 3342848 | tf_op jit(solution)/shard_map/dot_general | solution.py:61
  25.9 0.2 multiply_reduce_fusion
  26.1 0.1 multiply_convert_fusion.1
  26.2 0.5 convolution_convert_fusion.1
  26.7 25.8 %all_to_all.10 = bf16[8,48,1024]{2,1,0:T(8,128)(2,1)} all-to-all(bf16[8,48,1024]{2,1,0:T(8,128)(2,1)S(1)} %bitcast.95), channel_id=1, replica_groups=mesh['dp'=4,'seq'=4,'expert'=2] {'seq','expert'}, dimensions={0} | all-to-all | bytes 1572864 | tf_op jit(solution)/shard_map/all_to_all | solution.py:91
  52.5 0.0 all-gather.2.cloned.1.call-update
  52.6 0.0 reduce-scatter.2.cloned.1.call-start
  52.6 43.3 %all-gather.2.cloned.1.call-done = bf16[1536,1024]{1,0:T(8,128)(2,1)} async-done(((bf16[384,1024]{1,0:T(8,128)(2,1)}), bf16[1536,1024]{1,0:T(8,128)(2,1)}) %all-gather.2.cloned.1.call-update) | async-done | bytes 3145744 | tf_op jit(solution)/shard_map/all_gather | solution.py:93
  95.9 7.3 %fusion.3 = f32[1536,1024]{1,0:T(8,128)} fusion(bf16[1536,1024]{1,0:T(8,128)(2,1)} %all-gather.2.cloned.1.call-done, bf16[1,1024,1024]{2,1,0:T(8,128)(2,1)S(1)} %copy-done), kind=kOutput, calls=%fused_computation.4 | convolution fusion | flops 3221225472 | bytes 11534336 | tf_op jit(solution)/shard_map/dot_general | solution.py:94
  103.2 11.7 %convolution_convert_fusion = bf16[1536,1024]{1,0:T(8,128)(2,1)} fusion(f32[1536,1024]{1,0:T(8,128)} %fusion.3, bf16[1536,1024]{1,0:T(8,128)(2,1)} %all-gather.2.cloned.1.call-done, bf16[1,1024,1024]{2,1,0:T(8,128)(2,1)} %param.27, bf16[1,1024,1024]{2,1,0:T(8,128)(2,1)} %param.26), kind=kOutput, calls=%fused_computation.1 | convolution fusion | flops 6453460992 | bytes 16777216 | tf_op jit(solution)/shard_map/dot_general | solution.py:98
  114.9 0.0 reduce-scatter.2.cloned.1.call-update
  114.9 44.0 %reduce-scatter.2.cloned.1.call-done = bf16[384,1024]{1,0:T(8,128)(2,1)} async-done(((bf16[1536,1024]{1,0:T(8,128)(2,1)}), bf16[384,1024]{1,0:T(8,128)(2,1)}) %reduce-scatter.2.cloned.1.call-update) | async-done | bytes 786448 | tf_op jit(solution)/shard_map/reduce_scatter | solution.py:97
  158.9 5.3 %all-to-all-start.1 = ((bf16[8,48,1024]{2,1,0:T(8,128)(2,1)}), bf16[8,48,1024]{2,1,0:T(8,128)(2,1)S(1)}, u32[]{:S(2)}, u32[]{:S(2)}) async-start(bf16[8,48,1024]{2,1,0:T(8,128)(2,1)} %bitcast.96), calls=%async_computation.2 | async-start | bytes 1572864 | tf_op jit(solution)/shard_map/all_to_all | solution.py:106
  164.2 1.1 fusion.67
  165.4 19.0 %all-to-all-done.1 = bf16[8,48,1024]{2,1,0:T(8,128)(2,1)S(1)} async-done(((bf16[8,48,1024]{2,1,0:T(8,128)(2,1)}), bf16[8,48,1024]{2,1,0:T(8,128)(2,1)S(1)}, u32[]{:S(2)}, u32[]{:S(2)}) %all-to-all-start.1) | async-done | bytes 786464 | tf_op jit(solution)/shard_map/all_to_all | solution.py:106
  184.3 0.4 fusion.7
  184.7 1.1 fusion.9
  (28 shorter events, 0.2 us)
Async XLA Ops:
  6.5 89.4 %copy-start = (bf16[1,1024,1024]{2,1,0:T(8,128)(2,1)S(1)}, bf16[1,1024,1024]{2,1,0:T(8,128)(2,1)}, u32[]{:S(2)}) copy-start(bf16[1,1024,1024]{2,1,0:T(8,128)(2,1)} %param.25) | copy-start | bytes 6291460
  6.5 89.4 %all-gather.2.cloned.1.call-start = ((), (), s32[]{:S(2)}) async-start(), calls=%async_computation.3 | async-start | bytes 3932160 | tf_op jit(solution)/shard_map/all_gather | solution.py:93
  9.6 7.9 %copy-start.3 = (f32[31,1024]{1,0:T(8,128)S(1)}, f32[31,1024]{1,0:T(8,128)}, u32[]{:S(2)}) copy-start(f32[31,1024]{1,0:T(8,128)} %param.19) | copy-start | bytes 380932
  9.6 8.0 %copy-start.6 = (s32[1,128,2]{1,2,0:T(2,128)S(1)}, s32[1,128,2]{1,2,0:T(2,128)}, u32[]{:S(2)}) copy-start(s32[1,128,2]{1,2,0:T(2,128)} %param.16) | copy-start | bytes 3076
  9.6 11.2 %copy-start.2 = (bf16[1,128,1024]{2,1,0:T(8,128)(2,1)S(1)}, bf16[1,128,1024]{2,1,0:T(8,128)(2,1)}, u32[]{:S(2)}) copy-start(bf16[1,128,1024]{2,1,0:T(8,128)(2,1)} %param.14) | copy-start | bytes 786436
  9.6 11.2 %copy-start.7 = (f32[1024]{0:T(1024)S(1)}, f32[1024]{0:T(1024)}, u32[]{:S(2)}) copy-start(f32[1024]{0:T(1024)} %param.21) | copy-start | bytes 12292
  9.7 11.2 %copy-start.8 = (f32[1024]{0:T(1024)S(1)}, f32[1024]{0:T(1024)}, u32[]{:S(2)}) copy-start(f32[1024]{0:T(1024)} %param.20) | copy-start | bytes 12292
  13.0 5.0 %collective-permute-start = (bf16[15,1024]{1,0:T(8,128)(2,1)S(1)}, bf16[15,1024]{1,0:T(8,128)(2,1)S(1)}, u32[]{:S(2)}, u32[]{:S(2)}) collective-permute-start(bf16[15,1024]{1,0:T(8,128)(2,1)S(1)} %get-tuple-element.9), channel_id=1, source_target_pairs={{0,2},{2,4},{4,6},{1,3},{3,5},{5,7},{8,10},{10,12},{12,14},{9,11},... | collective-permute-start | bytes 92168 | tf_op jit(solution)/shard_map/ppermute | solution.py:14
  16.2 4.7 %collective-permute-start.1 = (bf16[15,1024]{1,0:T(8,128)(2,1)S(1)}, bf16[15,1024]{1,0:T(8,128)(2,1)S(1)}, u32[]{:S(2)}, u32[]{:S(2)}) collective-permute-start(bf16[15,1024]{1,0:T(8,128)(2,1)S(1)} %get-tuple-element.10), channel_id=1, source_target_pairs={{2,0},{4,2},{6,4},{3,1},{5,3},{7,5},{10,8},{12,10},{14,12},{11,9},... | collective-permute-start | bytes 92168 | tf_op jit(solution)/shard_map/ppermute | solution.py:15
  20.9 5.2 %copy-start.5 = (f32[1024]{0:T(1024)S(1)}, f32[1024]{0:T(1024)}, u32[]{:S(2)}) copy-start(f32[1024]{0:T(1024)} %param.23) | copy-start | bytes 12292
  26.2 26.3 %copy-start.1 = (bf16[128,1024]{1,0:T(8,128)(2,1)}, bf16[128,1024]{1,0:T(8,128)(2,1)S(1)}, u32[]{:S(2)}) copy-start(bf16[128,1024]{1,0:T(8,128)(2,1)S(1)} %multiply_convert_fusion.1) | copy-start | bytes 786436
  52.6 106.4 %reduce-scatter.2.cloned.1.call-start = ((), (), s32[]{:S(2)}) async-start(), calls=%async_computation.4 | async-start | bytes 3932160 | tf_op jit(solution)/shard_map/reduce_scatter | solution.py:97
  114.9 49.3 %copy-start.4 = (bf16[1024,8]{0,1:T(8,128)(2,1)S(1)}, bf16[1024,8]{0,1:T(8,128)(2,1)}, u32[]{:S(2)}) copy-start(bf16[1024,8]{0,1:T(8,128)(2,1)} %param.24) | copy-start | bytes 49156
  158.9 25.4 %all-to-all-start.1 = ((bf16[8,48,1024]{2,1,0:T(8,128)(2,1)}), bf16[8,48,1024]{2,1,0:T(8,128)(2,1)S(1)}, u32[]{:S(2)}, u32[]{:S(2)}) async-start(bf16[8,48,1024]{2,1,0:T(8,128)(2,1)} %bitcast.96), calls=%async_computation.2 | async-start | bytes 1572864 | tf_op jit(solution)/shard_map/all_to_all | solution.py:106
Sparse Core Ops, SparseCore 0:
  52.7 43.2 all-gather.1
  115.0 43.8 reduce-scatter.1
where the time goes:
time: 195 us; the launch traced here: 193 us
  waiting for transfers between devices  109 us (56%)
  matrix products  30 us (15%)
  blocking collectives  25.8 us (13%)
  between operations  14.4 us (7%)
  starting transfers between devices  9.81 us (5%)
  other arithmetic  3 us (2%)
    reduce_scatter x1, waiting for transfers between devices, local(): lax.psum_scatter(lax.dot_general(hidden, down_local, (((1,), (1,)), ((),...  44 us
    all_gather x1, waiting for transfers between devices, local(): lax.all_gather(arrived.reshape(-1, arrived_shape[2]), 'dp', axis=0, tiled...  43.3 us
    all_to_all x1, blocking collectives, local(): lax.all_to_all(outgoing, ('seq', 'expert'), split_axis=0, concat_axis=0,...  25.8 us
    all_to_all x1, waiting for transfers between devices, local(): lax.all_to_all(served, ('seq', 'expert'), split_axis=0, concat_axis=0, ti...  19 us
    dot_general x1, matrix products, local(): lax.dot_general(hidden, down_local, (((1,), (1,)), ((), ())), preferred_e...  11.7 us
    dot_general x1, matrix products, local(): jnp.dot(shard_rows, gate_local, preferred_element_type=jnp.float32)  7.26 us
    all_to_all x1, starting transfers between devices, local(): lax.all_to_all(served, ('seq', 'expert'), split_axis=0, concat_axis=0, ti...  5.27 us
    dot_general x1, matrix products, local(): jnp.dot(swished, point_out, preferred_element_type=jnp.float32)  4.95 us
  transfers between devices with their start and end apart: 5, of which 4 were waited for; matrix products, arithmetic and copies ran while one was open for 1% of the time, Pallas kernels for 0%

commit v1 on v0

--- a/solution.py
+++ b/solution.py
@@ -1,6 +1,9 @@
+import functools
 import jax
 import jax.numpy as jnp
 from jax import lax
+from jax.experimental import pallas as pl
+from jax.experimental.pallas import tpu as pltpu
 from jax.sharding import PartitionSpec as P
 
 
@@ -22,6 +25,305 @@
     center = values - jnp.mean(values, axis=-1, keepdims=True)
     spread = jnp.mean(center * center, axis=-1, keepdims=True)
     return center * lax.rsqrt(spread + 1e-05) * gain
+
+
+MESH = pl.DeviceIdType.MESH
+
+
+def kernel_fits(token_count, model_width, capacity, hidden):
+    sizes = (lax.axis_size("dp"), lax.axis_size("expert"))
+    return sizes == (4, 2) and capacity % 16 == 0 and model_width % 256 == 0 and hidden % 256 == 0
+
+
+def exchange_kernel(
+    seq,
+    out_hbm,
+    gate_hbm,
+    up_hbm,
+    down_hbm,
+    back,
+    sent,
+    gate,
+    up,
+    down,
+    rows,
+    part,
+    half,
+    joined,
+    sums,
+    total,
+    hidden,
+    load_sem,
+    own_sem,
+    z_send,
+    z_recv,
+    g_send,
+    g_recv,
+    r_send,
+    r_recv,
+    b_send,
+    b_recv,
+):
+    d, s, c = lax.axis_index("dp"), lax.axis_index("seq"), lax.axis_index("expert")
+    other = 1 - c
+    cap, width = rows.shape[3], rows.shape[4]
+    along_x = (d // 2 * 2 + (1 - d % 2), s, c)
+    along_y = ((d + 2) % 4, s, c)
+    loads = [
+        pltpu.make_async_copy(out_hbm, sent, load_sem.at[0]),
+        pltpu.make_async_copy(gate_hbm, gate, load_sem.at[1]),
+        pltpu.make_async_copy(up_hbm, up, load_sem.at[2]),
+        pltpu.make_async_copy(down_hbm, down, load_sem.at[3]),
+    ]
+    for load in loads:
+        load.start()
+
+    barrier = pltpu.get_barrier_semaphore()
+    peers = [along_x, along_y, (d, s, other)]
+    for k in range(1, seq):
+        peers += [(d, (s + k) % seq, 0), (d, (s + k) % seq, 1)]
+    for peer in peers:
+        pl.semaphore_signal(barrier, inc=1, device_id=peer, device_id_type=MESH)
+    pl.semaphore_wait(barrier, len(peers))
+    loads[0].wait()
+
+    def remote(src, dst, send, recv, to):
+        return pltpu.make_async_remote_copy(
+            src_ref=src, dst_ref=dst, send_sem=send, recv_sem=recv, device_id=to, device_id_type=MESH
+        )
+
+    def z_copy(k, q):
+        to = (s + seq - k) % seq
+        return remote(
+            sent.at[2 * to + q], rows.at[k, 0, c], z_send.at[k, q], z_recv.at[k, c], (d, to, q)
+        )
+
+    def z_arrival(k, q):
+        return remote(sent.at[0], rows.at[k, 0, q], z_send.at[k, q], z_recv.at[k, q], (d, s, other))
+
+    own = pltpu.make_async_copy(sent.at[2 * s + c], rows.at[0, 0, c], own_sem.at[0])
+    own.start()
+    z_copy(0, other).start()
+    for k in range(1, seq):
+        z_copy(k, 0).start()
+        z_copy(k, 1).start()
+
+    def g_x(k):
+        return remote(rows.at[k, 0], rows.at[k, 1], g_send.at[k, 0], g_recv.at[k, 0], along_x)
+
+    def g_y(k):
+        return remote(rows.at[k, 0], rows.at[k, 2], g_send.at[k, 1], g_recv.at[k, 1], along_y)
+
+    def g_xy(k):
+        return remote(rows.at[k, 1, 0], rows.at[k, 3, 0], g_send.at[k, 2], g_recv.at[k, 2], along_y)
+
+    def g_yx(k):
+        return remote(rows.at[k, 2, 1], rows.at[k, 3, 1], g_send.at[k, 3], g_recv.at[k, 3], along_x)
+
+    def r_xy(k):
+        return remote(part.at[k, 3, 0], half.at[k, 0], r_send.at[k, 0], r_recv.at[k, 0], along_x)
+
+    def r_yx(k):
+        return remote(part.at[k, 3, 1], half.at[k, 1], r_send.at[k, 1], r_recv.at[k, 1], along_y)
+
+    def r_x(k):
+        return remote(part.at[k, 1, 0], sums.at[k, 0, 0], r_send.at[k, 2], r_recv.at[k, 2], along_x)
+
+    def r_y(k):
+        return remote(part.at[k, 2, 1], sums.at[k, 1, 1], r_send.at[k, 3], r_recv.at[k, 3], along_y)
+
+    def r_x_joined(k):
+        return remote(joined.at[k, 0], sums.at[k, 0, 1], r_send.at[k, 4], r_recv.at[k, 4], along_x)
+
+    def r_y_joined(k):
+        return remote(joined.at[k, 1], sums.at[k, 1, 0], r_send.at[k, 5], r_recv.at[k, 5], along_y)
+
+    def b_copy(k, q):
+        return remote(
+            total.at[k, q], back.at[2 * s + c], b_send.at[k, q], b_recv.at[k, c], (d, (s + k) % seq, q)
+        )
+
+    def b_arrival(k, q):
+        e = 2 * ((s + seq - k) % seq) + q
+        return remote(total.at[k, q], back.at[e], b_send.at[k, q], b_recv.at[k, q], (d, s, other))
+
+    own_back = pltpu.make_async_copy(total.at[0, c], back.at[2 * s + c], own_sem.at[1])
+
+    def spread(k):
+        @pl.when(k == 0)
+        def _():
+            own.wait()
+            z_arrival(0, other).wait_recv()
+
+        @pl.when(k > 0)
+        def _():
+            z_arrival(k, 0).wait_recv()
+            z_arrival(k, 1).wait_recv()
+
+        g_x(k).start()
+        g_y(k).start()
+
+    def pass_on(k):
+        g_x(k).wait_recv()
+        g_xy(k).start()
+        g_y(k).wait_recv()
+        g_yx(k).start()
+
+    def experts(k):
+        g_xy(k).wait_recv()
+        g_yx(k).wait_recv()
+
+        @pl.when(k == 0)
+        def _():
+            for load in loads[1:]:
+                load.wait()
+
+        @pl.loop(0, hidden.shape[1] // 256)
+        def _(n):
+            columns = pl.ds(pl.multiple_of(n * 256, 256), 256)
+            x = rows[k].reshape(8 * cap, width)
+            g = jnp.dot(x, gate[:, columns], preferred_element_type=jnp.float32)
+            u = jnp.dot(x, up[:, columns], preferred_element_type=jnp.float32)
+            hidden[:, columns] = (g / (1.0 + jnp.exp(-g)) * u).astype(jnp.bfloat16)
+
+        @pl.loop(0, width // 256)
+        def _(n):
+            columns = pl.ds(pl.multiple_of(n * 256, 256), 256)
+            y = lax.dot_general(
+                hidden[...],
+                down[columns, :],
+                (((1,), (1,)), ((), ())),
+                preferred_element_type=jnp.float32,
+            )
+            part[k, :, :, :, columns] = y.astype(jnp.bfloat16).reshape(4, 2, cap, 256)
+
+        r_xy(k).start()
+        r_yx(k).start()
+        r_x(k).start()
+        r_y(k).start()
+
+    def join(k):
+        r_yx(k).wait_recv()
+        joined[k, 0] = (
+            part[k, 1, 1].astype(jnp.float32) + half[k, 1].astype(jnp.float32)
+        ).astype(jnp.bfloat16)
+        r_x_joined(k).start()
+        r_xy(k).wait_recv()
+        joined[k, 1] = (
+            part[k, 2, 0].astype(jnp.float32) + half[k, 0].astype(jnp.float32)
+        ).astype(jnp.bfloat16)
+        r_y_joined(k).start()
+
+    def give_back(k):
+        r_x(k).wait_recv()
+        r_y(k).wait_recv()
+        r_x_joined(k).wait_recv()
+        r_y_joined(k).wait_recv()
+        total[k] = (
+            part[k, 0].astype(jnp.float32)
+            + sums[k, 0].astype(jnp.float32)
+            + sums[k, 1].astype(jnp.float32)
+        ).astype(jnp.bfloat16)
+
+        @pl.when(k == 0)
+        def _():
+            own_back.start()
+            b_copy(0, other).start()
+
+        @pl.when(k > 0)
+        def _():
+            b_copy(k, 0).start()
+            b_copy(k, 1).start()
+
+    def at(k, step):
+        pl.when(jnp.logical_and(k >= 0, k < seq))(lambda: step(k))
+
+    @pl.loop(0, seq + 4)
+    def _(t):
+        at(t, spread)
+        at(t - 1, pass_on)
+        at(t - 2, experts)
+        at(t - 3, join)
+        at(t - 4, give_back)
+
+    own_back.wait()
+    b_arrival(0, other).wait_recv()
+    z_copy(0, other).wait_send()
+    b_copy(0, other).wait_send()
+    for k in range(1, seq):
+        for q in range(2):
+            b_arrival(k, q).wait_recv()
+            z_copy(k, q).wait_send()
+            b_copy(k, q).wait_send()
+
+    @pl.loop(0, seq)
+    def _(k):
+        for copy in (g_x, g_y, g_xy, g_yx, r_xy, r_yx, r_x, r_y, r_x_joined, r_y_joined):
+            copy(k).wait_send()
+
+
+def exchange(outgoing, gate_local, up_local, down_local):
+    experts, cap, width = outgoing.shape
+    seq, ff = lax.axis_size("seq"), gate_local.shape[1]
+    bf16, dma = jnp.bfloat16, pltpu.SemaphoreType.DMA
+    flops = 6 * 4 * experts * cap * width * ff
+    return pl.pallas_call(
+        functools.partial(exchange_kernel, seq),
+        out_shape=jax.ShapeDtypeStruct(outgoing.shape, bf16),
+        in_specs=[pl.BlockSpec(memory_space=pl.ANY)] * 4,
+        out_specs=pl.BlockSpec(memory_space=pltpu.VMEM),
+        scratch_shapes=[
+            pltpu.VMEM(outgoing.shape, bf16),
+            pltpu.VMEM(gate_local.shape, bf16),
+            pltpu.VMEM(up_local.shape, bf16),
+            pltpu.VMEM(down_local.shape, bf16),
+            pltpu.VMEM((seq, 4, 2, cap, width), bf16),
+            pltpu.VMEM((seq, 4, 2, cap, width), bf16),
+            pltpu.VMEM((seq, 2, cap, width), bf16),
+            pltpu.VMEM((seq, 2, cap, width), bf16),
+            pltpu.VMEM((seq, 2, 2, cap, width), bf16),
+            pltpu.VMEM((seq, 2, cap, width), bf16),
+            pltpu.VMEM((8 * cap, ff), bf16),
+            dma((4,)),
+            dma((2,)),
+            dma((seq, 2)),
+            dma((seq, 2)),
+            dma((seq, 4)),
+            dma((seq, 4)),
+            dma((seq, 6)),
+            dma((seq, 6)),
+            dma((seq, 2)),
+            dma((seq, 2)),
+        ],
+        compiler_params=pltpu.CompilerParams(
+            collective_id=0, has_side_effects=True, vmem_limit_bytes=40 << 20
+        ),
+        cost_estimate=pl.CostEstimate(
+            flops=flops, bytes_accessed=6 * width * ff, transcendentals=4 * experts * cap * ff
+        ),
+    )(outgoing, gate_local, up_local, down_local)
+
+
+def exchange_plain(outgoing, gate_local, up_local, down_local):
+    arrived = lax.all_to_all(outgoing, ("seq", "expert"), split_axis=0, concat_axis=0, tiled=True)
+    arrived_shape = arrived.shape
+    shard_rows = lax.all_gather(arrived.reshape(-1, arrived_shape[2]), "dp", axis=0, tiled=True)
+    gate_part = jnp.dot(shard_rows, gate_local, preferred_element_type=jnp.float32)
+    up_part = jnp.dot(shard_rows, up_local, preferred_element_type=jnp.float32)
+    hidden = (jax.nn.silu(gate_part) * up_part).astype(jnp.bfloat16)
+    summed = lax.psum_scatter(
+        lax.dot_general(
+            hidden, down_local, (((1,), (1,)), ((), ())), preferred_element_type=jnp.float32
+        ).astype(jnp.bfloat16),
+        "dp",
+        scatter_dimension=0,
+        tiled=True,
+    )
+    served = summed.reshape(arrived_shape)
+    returned_rows = lax.all_to_all(
+        served, ("seq", "expert"), split_axis=0, concat_axis=0, tiled=True
+    )
+    return returned_rows
 
 
 def local(
@@ -75,7 +377,11 @@
     weight_one = jax.nn.sigmoid(logit_one - logit_two)
     weight_two = jax.nn.sigmoid(logit_two - logit_one)
     both = pick_one + pick_two
-    earlier = jnp.cumsum(both, axis=0) - both
+    rank = jnp.arange(token_count, dtype=jnp.int32)
+    lower = (rank[:, None] > rank[None, :]).astype(jnp.bfloat16)
+    earlier = jnp.dot(
+        lower, both.astype(jnp.bfloat16), preferred_element_type=jnp.float32
+    ).astype(jnp.int32)
     place_one = choice_ids[:, 0] * capacity + jnp.sum(earlier * pick_one, axis=1)
     place_two = choice_ids[:, 1] * capacity + jnp.sum(earlier * pick_two, axis=1)
     slot_ids = jnp.arange(expert_count * capacity, dtype=jnp.int32)
@@ -88,24 +394,10 @@
     gate_local = gate_weight[0]
     up_local = up_weight[0]
     down_local = down_weight[0]
-    arrived = lax.all_to_all(outgoing, ("seq", "expert"), split_axis=0, concat_axis=0, tiled=True)
-    arrived_shape = arrived.shape
-    shard_rows = lax.all_gather(arrived.reshape(-1, arrived_shape[2]), "dp", axis=0, tiled=True)
-    gate_part = jnp.dot(shard_rows, gate_local, preferred_element_type=jnp.float32)
-    up_part = jnp.dot(shard_rows, up_local, preferred_element_type=jnp.float32)
-    hidden = (jax.nn.silu(gate_part) * up_part).astype(jnp.bfloat16)
-    summed = lax.psum_scatter(
-        lax.dot_general(
-            hidden, down_local, (((1,), (1,)), ((), ())), preferred_element_type=jnp.float32
-        ).astype(jnp.bfloat16),
-        "dp",
-        scatter_dimension=0,
-        tiled=True,
-    )
-    served = summed.reshape(arrived_shape)
-    returned_rows = lax.all_to_all(
-        served, ("seq", "expert"), split_axis=0, concat_axis=0, tiled=True
-    )
+    if kernel_fits(token_count, model_width, capacity, gate_local.shape[1]):
+        returned_rows = exchange(outgoing, gate_local, up_local, down_local)
+    else:
+        returned_rows = exchange_plain(outgoing, gate_local, up_local, down_local)
     returned_rows = returned_rows.reshape(expert_count * capacity, model_width)
     from_one = jnp.dot(slot_one, returned_rows, preferred_element_type=jnp.float32)
     from_two = jnp.dot(slot_two, returned_rows, preferred_element_type=jnp.float32)

time: 195 us -> 94.8 us (0.49)
  the two profiles are of different devices: /device:TPU:3 before, /device:TPU:0 now
where the time goes in v1:
time: 94.8 us; the launch traced here: 94.6 us
  Pallas kernels  71.5 us (75%)
  matrix products  8.12 us (9%)
  starting transfers between devices  6.22 us (7%)
  waiting for transfers between devices  4.18 us (4%)
  other arithmetic  2.8 us (3%)
  between operations  1.08 us (1%)
    pallas_call x1, Pallas kernels, exchange(): pl.pallas_call(functools.partial(exchange_kernel, seq), out_shape=jax.Sha...  71.5 us
    ppermute x1, starting transfers between devices, padded_2(): before = lax.ppermute(last, axis, up)  4.93 us
    ppermute x1, waiting for transfers between devices, padded_2(): after = lax.ppermute(initial, axis, down)  4.18 us
    dot_general x1, matrix products, local(): lifted = jnp.dot(conv_in, point_in, preferred_element_type=jnp.float32)  3.14 us
    dot_general x1, matrix products, local(): jnp.dot(swished, point_out, preferred_element_type=jnp.float32)  2.76 us
  transfers between devices with their start and end apart: 2, of which 1 were waited for; matrix products, arithmetic and copies ran while one was open for 0% of the time, Pallas kernels for 0%

profile of v1, /device:TPU:0, one launch (start us, length us, event | category | flops | bytes accessed | tf_op | source)
XLA Modules:
  0.0 94.6 jit_solution(9699192454817868128)
XLA Ops:
  0.8 1.1 %convert_reduce_fusion = f32[128]{0:T(128)S(1)} fusion(bf16[1,128,1024]{2,1,0:T(8,128)(2,1)} %param.14), kind=kLoop, calls=%fused_computation.38 | loop fusion | flops 262016 | bytes 262656 | tf_op jit(solution)/shard_map/reduce_sum | solution.py:25
  1.9 1.2 %fusion.8 = f32[128]{0:T(128)S(1)} fusion(bf16[1,128,1024]{2,1,0:T(8,128)(2,1)} %param.14, f32[128]{0:T(128)S(1)} %broadcast_multiply_fusion.1), kind=kLoop, calls=%fused_computation.43 | loop fusion | flops 524160 | bytes 263168 | tf_op jit(solution)/shard_map/reduce_sum | solution.py:26
  3.1 0.0 copy-start.5
  3.1 0.0 copy-start.8
  3.1 0.0 copy-start.4
  3.1 0.0 copy-start.9
  3.1 0.0 copy-start.10
  3.1 3.1 %fusion.17 = f32[128,2048]{1,0:T(8,128)S(1)} fusion(bf16[1024,2048]{1,0:T(8,128)(2,1)} %param.18, bf16[1,128,1024]{2,1,0:T(8,128)(2,1)} %param.14, f32[1024]{0:T(1024)} %param.17, f32[128]{0:T(128)S(1)} %add_rsqrt_fusion.1, f32[128]{0:T(128)S(1)} %broadcast_multiply_fusion.1), kind=kOutput, calls=%fused_computation.56 | convolution fusion | flops 537526272 | bytes 5510144 | tf_op jit(solution)/shard_map/dot_general | solution.py:351
  6.3 0.2 fusion.16
  6.5 4.9 %collective-permute-start = (bf16[15,1024]{1,0:T(8,128)(2,1)S(1)}, bf16[15,1024]{1,0:T(8,128)(2,1)S(1)}, u32[]{:S(2)}, u32[]{:S(2)}) collective-permute-start(bf16[15,1024]{1,0:T(8,128)(2,1)S(1)} %get-tuple-element.9), channel_id=1, source_target_pairs={{0,2},{2,4},{4,6},{1,3},{3,5},{5,7},{8,10},{10,12},{12,14},{9,11},... | collective-permute-start | bytes 92168 | tf_op jit(solution)/shard_map/ppermute | solution.py:17
  11.4 1.3 %collective-permute-start.1 = (bf16[15,1024]{1,0:T(8,128)(2,1)S(1)}, bf16[15,1024]{1,0:T(8,128)(2,1)S(1)}, u32[]{:S(2)}, u32[]{:S(2)}) collective-permute-start(bf16[15,1024]{1,0:T(8,128)(2,1)S(1)} %get-tuple-element.10), channel_id=1, source_target_pairs={{2,0},{4,2},{6,4},{3,1},{5,3},{7,5},{10,8},{12,10},{14,12},{11,9},... | collective-permute-start | bytes 92168 | tf_op jit(solution)/shard_map/ppermute | solution.py:18
  12.7 0.0 copy-done.5
  12.8 0.1 fusion.72
  12.9 0.2 select_reduce_fusion.1
  13.0 0.0 collective-permute-done
  13.0 4.2 %collective-permute-done.1 = bf16[15,1024]{1,0:T(8,128)(2,1)S(1)} collective-permute-done((bf16[15,1024]{1,0:T(8,128)(2,1)S(1)}, bf16[15,1024]{1,0:T(8,128)(2,1)S(1)}, u32[]{:S(2)}, u32[]{:S(2)}) %collective-permute-start.1) | collective-permute-done | bytes 30752 | tf_op jit(solution)/shard_map/ppermute | solution.py:18
  17.2 0.0 copy-done.4
  17.2 0.0 copy-start.7
  17.2 0.0 copy-start.6
  17.3 0.0 copy-start.2
  17.3 0.0 copy-start.3
  17.3 2.8 %fusion.74 = (f32[128]{0:T(128)S(1)}, f32[128,1024]{1,0:T(8,128)S(1)}) fusion(bf16[1024,1024]{1,0:T(8,128)(2,1)S(1)} %copy-done, bf16[128,1024]{1,0:T(8,128)(2,1)S(1)} %fusion.16, bf16[15,1024]{1,0:T(8,128)(2,1)S(1)} %collective-permute-done.1, bf16[15,1024]{1,0:T(8,128)(2,1)S(1)} %collective-permute-done, f32[1024]{0:T(1024)S(1)} %copy-done.9, ...), kind=kOutput, calls=%fused_computation.152 | convolution fusion | flops 293601152 | bytes 3342848 | tf_op jit(solution)/shard_map/dot_general | solution.py:363
  20.1 0.2 multiply_reduce_fusion
  20.3 0.1 multiply_convert_fusion
  20.4 0.2 fusion.62
  20.6 0.5 convolution_convert_fusion
  21.1 0.0 copy-done.2
  21.1 0.0 copy-done.3
  21.2 0.5 copy-done.1
  21.6 71.5 %shard_map.136 = bf16[8,48,1024]{2,1,0:T(8,128)(2,1)S(1)} custom-call(bf16[8,48,1024]{2,1,0:T(8,128)(2,1)S(1)} %bitcast.83, bf16[1024,1024]{1,0:T(8,128)(2,1)S(1)} %bitcast.84, bf16[1024,1024]{1,0:T(8,128)(2,1)S(1)} %bitcast.85, bf16[1024,1024]{1,0:T(8,128)(2,1)S(1)} %bitcast.86), custom_call_target="tpu_custom_call" | custom-call | flops 9663676416 | bytes 6291456 | tf_op jit(solution)/shard_map/pallas_call | solution.py:270
  93.2 0.4 fusion.2
  93.5 1.1 %fusion.4 = bf16[1,128,1024]{2,1,0:T(8,128)(2,1)} fusion(f32[128,1024]{1,0:T(8,128)S(1)} %fusion.2, bf16[384,1024]{1,0:T(8,128)(2,1)S(1)} %bitcast.82, f32[128]{0:T(128)S(1)} %get-tuple-element.42, f32[128]{0:T(128)S(1)} %compare_convert_fusion, s32[128]{0:T(128)S(1)} %get-tuple-element.45), kind=kOutput, calls=%fused_computation.36 | convolution fusion | flops 101236736 | bytes 1574400 | tf_op jit(solution)/shard_map/dot_general | solution.py:403
  (18 shorter events, 0.1 us)
Async XLA Ops:
  0.0 17.2 %copy-start = (bf16[1024,1024]{1,0:T(8,128)(2,1)S(1)}, bf16[1024,1024]{1,0:T(8,128)(2,1)}, u32[]{:S(2)}) copy-start(bf16[1024,1024]{1,0:T(8,128)(2,1)} %param.22) | copy-start | bytes 6291460
  3.1 9.6 %copy-start.5 = (f32[31,1024]{1,0:T(8,128)S(1)}, f32[31,1024]{1,0:T(8,128)}, u32[]{:S(2)}) copy-start(f32[31,1024]{1,0:T(8,128)} %param.19) | copy-start | bytes 380932
  3.1 9.7 %copy-start.8 = (s32[1,128,2]{1,2,0:T(2,128)S(1)}, s32[1,128,2]{1,2,0:T(2,128)}, u32[]{:S(2)}) copy-start(s32[1,128,2]{1,2,0:T(2,128)} %param.16) | copy-start | bytes 3076
  3.1 14.1 %copy-start.4 = (bf16[1,128,1024]{2,1,0:T(8,128)(2,1)S(1)}, bf16[1,128,1024]{2,1,0:T(8,128)(2,1)}, u32[]{:S(2)}) copy-start(bf16[1,128,1024]{2,1,0:T(8,128)(2,1)} %param.14) | copy-start | bytes 786436
  3.1 14.1 %copy-start.9 = (f32[1024]{0:T(1024)S(1)}, f32[1024]{0:T(1024)}, u32[]{:S(2)}) copy-start(f32[1024]{0:T(1024)} %param.21) | copy-start | bytes 12292
  3.1 14.1 %copy-start.10 = (f32[1024]{0:T(1024)S(1)}, f32[1024]{0:T(1024)}, u32[]{:S(2)}) copy-start(f32[1024]{0:T(1024)} %param.20) | copy-start | bytes 12292
  6.5 6.6 %collective-permute-start = (bf16[15,1024]{1,0:T(8,128)(2,1)S(1)}, bf16[15,1024]{1,0:T(8,128)(2,1)S(1)}, u32[]{:S(2)}, u32[]{:S(2)}) collective-permute-start(bf16[15,1024]{1,0:T(8,128)(2,1)S(1)} %get-tuple-element.9), channel_id=1, source_target_pairs={{0,2},{2,4},{4,6},{1,3},{3,5},{5,7},{8,10},{10,12},{12,14},{9,11},... | collective-permute-start | bytes 92168 | tf_op jit(solution)/shard_map/ppermute | solution.py:17
  11.4 5.8 %collective-permute-start.1 = (bf16[15,1024]{1,0:T(8,128)(2,1)S(1)}, bf16[15,1024]{1,0:T(8,128)(2,1)S(1)}, u32[]{:S(2)}, u32[]{:S(2)}) collective-permute-start(bf16[15,1024]{1,0:T(8,128)(2,1)S(1)} %get-tuple-element.10), channel_id=1, source_target_pairs={{2,0},{4,2},{6,4},{3,1},{5,3},{7,5},{10,8},{12,10},{14,12},{11,9},... | collective-permute-start | bytes 92168 | tf_op jit(solution)/shard_map/ppermute | solution.py:18
  17.2 3.0 %copy-start.7 = (f32[1024]{0:T(1024)S(1)}, f32[1024]{0:T(1024)}, u32[]{:S(2)}) copy-start(f32[1024]{0:T(1024)} %param.23) | copy-start | bytes 12292
  17.2 3.2 %copy-start.6 = (bf16[1024,8]{0,1:T(8,128)(2,1)S(1)}, bf16[1024,8]{0,1:T(8,128)(2,1)}, u32[]{:S(2)}) copy-start(bf16[1024,8]{0,1:T(8,128)(2,1)} %param.24) | copy-start | bytes 49156
  17.3 3.9 %copy-start.2 = (bf16[1,1024,1024]{2,1,0:T(8,128)(2,1)S(1)}, bf16[1,1024,1024]{2,1,0:T(8,128)(2,1)}, u32[]{:S(2)}) copy-start(bf16[1,1024,1024]{2,1,0:T(8,128)(2,1)} %param.26) | copy-start | bytes 6291460
  17.3 3.9 %copy-start.3 = (bf16[1,1024,1024]{2,1,0:T(8,128)(2,1)S(1)}, bf16[1,1024,1024]{2,1,0:T(8,128)(2,1)}, u32[]{:S(2)}) copy-start(bf16[1,1024,1024]{2,1,0:T(8,128)(2,1)} %param.27) | copy-start | bytes 6291460
  20.0 1.6 %copy-start.1 = (bf16[1,1024,1024]{2,1,0:T(8,128)(2,1)S(1)}, bf16[1,1024,1024]{2,1,0:T(8,128)(2,1)}, u32[]{:S(2)}) copy-start(bf16[1,1024,1024]{2,1,0:T(8,128)(2,1)} %param.25) | copy-start | bytes 6291460

commit v2 on v1

--- a/solution.py
+++ b/solution.py
@@ -104,9 +104,8 @@
     own = pltpu.make_async_copy(sent.at[2 * s + c], rows.at[0, 0, c], own_sem.at[0])
     own.start()
     z_copy(0, other).start()
-    for k in range(1, seq):
-        z_copy(k, 0).start()
-        z_copy(k, 1).start()
+    z_copy(1, 0).start()
+    z_copy(1, 1).start()
 
     def g_x(k):
         return remote(rows.at[k, 0], rows.at[k, 1], g_send.at[k, 0], g_recv.at[k, 0], along_x)
@@ -149,19 +148,29 @@
 
     own_back = pltpu.make_async_copy(total.at[0, c], back.at[2 * s + c], own_sem.at[1])
 
-    def spread(k):
-        @pl.when(k == 0)
+    def nth(t):
+        return t + t // 2 - 2 * (t // 3) if seq == 4 else t
+
+    def spread(t):
+        k = nth(t)
+
+        @pl.when(t == 0)
         def _():
             own.wait()
             z_arrival(0, other).wait_recv()
 
-        @pl.when(k > 0)
+        @pl.when(t > 0)
         def _():
             z_arrival(k, 0).wait_recv()
             z_arrival(k, 1).wait_recv()
 
         g_x(k).start()
         g_y(k).start()
+
+        @pl.when(jnp.logical_and(t > 0, t + 1 < seq))
+        def _():
+            z_copy(nth(t + 1), 0).start()
+            z_copy(nth(t + 1), 1).start()
 
     def pass_on(k):
         g_x(k).wait_recv()
@@ -173,7 +182,7 @@
         g_xy(k).wait_recv()
         g_yx(k).wait_recv()
 
-        @pl.when(k == 0)
+        @pl.when(k == nth(1))
         def _():
             for load in loads[1:]:
                 load.wait()
@@ -235,16 +244,19 @@
             b_copy(k, 0).start()
             b_copy(k, 1).start()
 
-    def at(k, step):
-        pl.when(jnp.logical_and(k >= 0, k < seq))(lambda: step(k))
-
-    @pl.loop(0, seq + 4)
+    def at(t, step):
+        pl.when(jnp.logical_and(t >= 0, t < seq))(lambda: step(t))
+
+    def late(step):
+        return lambda t: step(nth((t + 1) % seq))
+
+    @pl.loop(0, seq + 5)
     def _(t):
+        at(t - 1, lambda i: pass_on(nth(i)))
         at(t, spread)
-        at(t - 1, pass_on)
-        at(t - 2, experts)
-        at(t - 3, join)
-        at(t - 4, give_back)
+        at(t - 2, late(experts))
+        at(t - 3, late(join))
+        at(t - 4, late(give_back))
 
     own_back.wait()
     b_arrival(0, other).wait_recv()

time: 94.8 us -> 93.7 us (0.988)
  the two profiles are of different devices: /device:TPU:0 before, /device:TPU:3 now
where the time goes in v2:
time: 93.7 us; the launch traced here: 92.8 us
  Pallas kernels  72.6 us (77%)
  matrix products  8.12 us (9%)
  starting transfers between devices  4.5 us (5%)
  waiting for transfers between devices  3.03 us (3%)
  other arithmetic  2.8 us (3%)
  between operations  1.08 us (1%)
    pallas_call x1, Pallas kernels, exchange(): pl.pallas_call(functools.partial(exchange_kernel, seq), out_shape=jax.Sha...  72.6 us
    ppermute x1, starting transfers between devices, padded_2(): before = lax.ppermute(last, axis, up)  3.2 us
    dot_general x1, matrix products, local(): lifted = jnp.dot(conv_in, point_in, preferred_element_type=jnp.float32)  3.14 us
    ppermute x1, waiting for transfers between devices, padded_2(): after = lax.ppermute(initial, axis, down)  3.03 us
    dot_general x1, matrix products, local(): jnp.dot(swished, point_out, preferred_element_type=jnp.float32)  2.75 us
  transfers between devices with their start and end apart: 2, of which 1 were waited for; matrix products, arithmetic and copies ran while one was open for 0% of the time, Pallas kernels for 0%

profile of v2, /device:TPU:3, one launch (start us, length us, event | category | flops | bytes accessed | tf_op | source)
XLA Modules:
  0.0 92.8 jit_solution(8370411691188332396)
XLA Ops:
  0.0 0.0 copy-start
  0.8 1.1 %convert_reduce_fusion = f32[128]{0:T(128)S(1)} fusion(bf16[1,128,1024]{2,1,0:T(8,128)(2,1)} %param.14), kind=kLoop, calls=%fused_computation.38 | loop fusion | flops 262016 | bytes 262656 | tf_op jit(solution)/shard_map/reduce_sum | solution.py:25
  1.9 1.2 %fusion.8 = f32[128]{0:T(128)S(1)} fusion(bf16[1,128,1024]{2,1,0:T(8,128)(2,1)} %param.14, f32[128]{0:T(128)S(1)} %broadcast_multiply_fusion.1), kind=kLoop, calls=%fused_computation.43 | loop fusion | flops 524160 | bytes 263168 | tf_op jit(solution)/shard_map/reduce_sum | solution.py:26
  3.1 0.0 copy-start.5
  3.1 0.0 copy-start.8
  3.1 0.0 copy-start.4
  3.1 0.0 copy-start.9
  3.1 0.0 copy-start.10
  3.1 3.1 %fusion.17 = f32[128,2048]{1,0:T(8,128)S(1)} fusion(bf16[1024,2048]{1,0:T(8,128)(2,1)} %param.18, bf16[1,128,1024]{2,1,0:T(8,128)(2,1)} %param.14, f32[1024]{0:T(1024)} %param.17, f32[128]{0:T(128)S(1)} %add_rsqrt_fusion.1, f32[128]{0:T(128)S(1)} %broadcast_multiply_fusion.1), kind=kOutput, calls=%fused_computation.56 | convolution fusion | flops 537526272 | bytes 5510144 | tf_op jit(solution)/shard_map/dot_general | solution.py:363
  6.3 0.2 fusion.16
  6.5 3.2 %collective-permute-start = (bf16[15,1024]{1,0:T(8,128)(2,1)S(1)}, bf16[15,1024]{1,0:T(8,128)(2,1)S(1)}, u32[]{:S(2)}, u32[]{:S(2)}) collective-permute-start(bf16[15,1024]{1,0:T(8,128)(2,1)S(1)} %get-tuple-element.9), channel_id=1, source_target_pairs={{0,2},{2,4},{4,6},{1,3},{3,5},{5,7},{8,10},{10,12},{12,14},{9,11},... | collective-permute-start | bytes 92168 | tf_op jit(solution)/shard_map/ppermute | solution.py:17
  9.7 1.3 %collective-permute-start.1 = (bf16[15,1024]{1,0:T(8,128)(2,1)S(1)}, bf16[15,1024]{1,0:T(8,128)(2,1)S(1)}, u32[]{:S(2)}, u32[]{:S(2)}) collective-permute-start(bf16[15,1024]{1,0:T(8,128)(2,1)S(1)} %get-tuple-element.10), channel_id=1, source_target_pairs={{2,0},{4,2},{6,4},{3,1},{5,3},{7,5},{10,8},{12,10},{14,12},{11,9},... | collective-permute-start | bytes 92168 | tf_op jit(solution)/shard_map/ppermute | solution.py:18
  11.0 0.1 fusion.72
  11.1 0.0 copy-done.8
  11.1 0.2 select_reduce_fusion.1
  11.3 0.0 collective-permute-done
  11.3 3.0 %collective-permute-done.1 = bf16[15,1024]{1,0:T(8,128)(2,1)S(1)} collective-permute-done((bf16[15,1024]{1,0:T(8,128)(2,1)S(1)}, bf16[15,1024]{1,0:T(8,128)(2,1)S(1)}, u32[]{:S(2)}, u32[]{:S(2)}) %collective-permute-start.1) | collective-permute-done | bytes 30752 | tf_op jit(solution)/shard_map/ppermute | solution.py:18
  14.3 0.0 copy-done
  14.4 0.0 copy-start.7
  14.4 0.0 copy-start.6
  14.4 0.0 copy-start.2
  14.4 0.0 copy-start.3
  14.4 2.8 %fusion.74 = (f32[128]{0:T(128)S(1)}, f32[128,1024]{1,0:T(8,128)S(1)}) fusion(bf16[1024,1024]{1,0:T(8,128)(2,1)S(1)} %copy-done, bf16[128,1024]{1,0:T(8,128)(2,1)S(1)} %fusion.16, bf16[15,1024]{1,0:T(8,128)(2,1)S(1)} %collective-permute-done.1, bf16[15,1024]{1,0:T(8,128)(2,1)S(1)} %collective-permute-done, f32[1024]{0:T(1024)S(1)} %copy-done.9, ...), kind=kOutput, calls=%fused_computation.152 | convolution fusion | flops 293601152 | bytes 3342848 | tf_op jit(solution)/shard_map/dot_general | solution.py:375
  17.2 0.2 multiply_reduce_fusion
  17.4 0.1 multiply_convert_fusion
  17.5 0.0 copy-done.6
  17.6 0.2 fusion.62
  17.8 0.5 convolution_convert_fusion
  18.3 0.5 copy-done.1
  18.8 72.6 %shard_map.136 = bf16[8,48,1024]{2,1,0:T(8,128)(2,1)S(1)} custom-call(bf16[8,48,1024]{2,1,0:T(8,128)(2,1)S(1)} %bitcast.83, bf16[1024,1024]{1,0:T(8,128)(2,1)S(1)} %bitcast.84, bf16[1024,1024]{1,0:T(8,128)(2,1)S(1)} %bitcast.85, bf16[1024,1024]{1,0:T(8,128)(2,1)S(1)} %bitcast.86), custom_call_target="tpu_custom_call" | custom-call | flops 9663676416 | bytes 6291456 | tf_op jit(solution)/shard_map/pallas_call | solution.py:282
  91.4 0.4 fusion.2
  91.8 1.1 %fusion.4 = bf16[1,128,1024]{2,1,0:T(8,128)(2,1)} fusion(f32[128,1024]{1,0:T(8,128)S(1)} %fusion.2, bf16[384,1024]{1,0:T(8,128)(2,1)S(1)} %bitcast.82, f32[128]{0:T(128)S(1)} %get-tuple-element.42, f32[128]{0:T(128)S(1)} %compare_convert_fusion, s32[128]{0:T(128)S(1)} %get-tuple-element.45), kind=kOutput, calls=%fused_computation.36 | convolution fusion | flops 101236736 | bytes 1574400 | tf_op jit(solution)/shard_map/dot_general | solution.py:415
  (18 shorter events, 0.1 us)
Async XLA Ops:
  0.0 14.3 %copy-start = (bf16[1024,1024]{1,0:T(8,128)(2,1)S(1)}, bf16[1024,1024]{1,0:T(8,128)(2,1)}, u32[]{:S(2)}) copy-start(bf16[1024,1024]{1,0:T(8,128)(2,1)} %param.22) | copy-start | bytes 6291460
  3.1 7.9 %copy-start.5 = (f32[31,1024]{1,0:T(8,128)S(1)}, f32[31,1024]{1,0:T(8,128)}, u32[]{:S(2)}) copy-start(f32[31,1024]{1,0:T(8,128)} %param.19) | copy-start | bytes 380932
  3.1 8.0 %copy-start.8 = (s32[1,128,2]{1,2,0:T(2,128)S(1)}, s32[1,128,2]{1,2,0:T(2,128)}, u32[]{:S(2)}) copy-start(s32[1,128,2]{1,2,0:T(2,128)} %param.16) | copy-start | bytes 3076
  3.1 11.2 %copy-start.4 = (bf16[1,128,1024]{2,1,0:T(8,128)(2,1)S(1)}, bf16[1,128,1024]{2,1,0:T(8,128)(2,1)}, u32[]{:S(2)}) copy-start(bf16[1,128,1024]{2,1,0:T(8,128)(2,1)} %param.14) | copy-start | bytes 786436
  3.1 11.2 %copy-start.9 = (f32[1024]{0:T(1024)S(1)}, f32[1024]{0:T(1024)}, u32[]{:S(2)}) copy-start(f32[1024]{0:T(1024)} %param.21) | copy-start | bytes 12292
  3.1 11.2 %copy-start.10 = (f32[1024]{0:T(1024)S(1)}, f32[1024]{0:T(1024)}, u32[]{:S(2)}) copy-start(f32[1024]{0:T(1024)} %param.20) | copy-start | bytes 12292
  6.5 4.8 %collective-permute-start = (bf16[15,1024]{1,0:T(8,128)(2,1)S(1)}, bf16[15,1024]{1,0:T(8,128)(2,1)S(1)}, u32[]{:S(2)}, u32[]{:S(2)}) collective-permute-start(bf16[15,1024]{1,0:T(8,128)(2,1)S(1)} %get-tuple-element.9), channel_id=1, source_target_pairs={{0,2},{2,4},{4,6},{1,3},{3,5},{5,7},{8,10},{10,12},{12,14},{9,11},... | collective-permute-start | bytes 92168 | tf_op jit(solution)/shard_map/ppermute | solution.py:17
  9.7 4.7 %collective-permute-start.1 = (bf16[15,1024]{1,0:T(8,128)(2,1)S(1)}, bf16[15,1024]{1,0:T(8,128)(2,1)S(1)}, u32[]{:S(2)}, u32[]{:S(2)}) collective-permute-start(bf16[15,1024]{1,0:T(8,128)(2,1)S(1)} %get-tuple-element.10), channel_id=1, source_target_pairs={{2,0},{4,2},{6,4},{3,1},{5,3},{7,5},{10,8},{12,10},{14,12},{11,9},... | collective-permute-start | bytes 92168 | tf_op jit(solution)/shard_map/ppermute | solution.py:18
  14.4 3.0 %copy-start.7 = (f32[1024]{0:T(1024)S(1)}, f32[1024]{0:T(1024)}, u32[]{:S(2)}) copy-start(f32[1024]{0:T(1024)} %param.23) | copy-start | bytes 12292
  14.4 3.2 %copy-start.6 = (bf16[1024,8]{0,1:T(8,128)(2,1)S(1)}, bf16[1024,8]{0,1:T(8,128)(2,1)}, u32[]{:S(2)}) copy-start(bf16[1024,8]{0,1:T(8,128)(2,1)} %param.24) | copy-start | bytes 49156
  14.4 3.9 %copy-start.2 = (bf16[1,1024,1024]{2,1,0:T(8,128)(2,1)S(1)}, bf16[1,1024,1024]{2,1,0:T(8,128)(2,1)}, u32[]{:S(2)}) copy-start(bf16[1,1024,1024]{2,1,0:T(8,128)(2,1)} %param.26) | copy-start | bytes 6291460
  14.4 3.9 %copy-start.3 = (bf16[1,1024,1024]{2,1,0:T(8,128)(2,1)S(1)}, bf16[1,1024,1024]{2,1,0:T(8,128)(2,1)}, u32[]{:S(2)}) copy-start(bf16[1,1024,1024]{2,1,0:T(8,128)(2,1)} %param.27) | copy-start | bytes 6291460
  17.2 1.6 %copy-start.1 = (bf16[1,1024,1024]{2,1,0:T(8,128)(2,1)S(1)}, bf16[1,1024,1024]{2,1,0:T(8,128)(2,1)}, u32[]{:S(2)}) copy-start(bf16[1,1024,1024]{2,1,0:T(8,128)(2,1)} %param.25) | copy-start | bytes 6291460

commit v3 on v2

--- a/solution.py
+++ b/solution.py
@@ -7,17 +7,80 @@
 from jax.sharding import PartitionSpec as P
 
 
-def padded_2(x, sides, width):
-    for axis, dim in sides:
-        size, length = (lax.axis_size(axis), x.shape[dim])
-        up = [(i, (i + 1) % size) for i in range(size - 1)]
-        down = [(j, i) for i, j in up]
-        last = lax.slice_in_dim(x, length - width, length, axis=dim)
-        initial = lax.slice_in_dim(x, 0, width, axis=dim)
-        before = lax.ppermute(last, axis, up)
-        after = lax.ppermute(initial, axis, down)
-        x = jnp.concatenate([before, x, after], axis=dim)
-    return x
+def halo_kernel(seq, x, before, after, send_sem, recv_sem):
+    d, s, c = lax.axis_index("dp"), lax.axis_index("seq"), lax.axis_index("expert")
+    width, rows = before.shape[0], x.shape[0]
+    left, right = (d, (s + seq - 1) % seq, c), (d, (s + 1) % seq, c)
+    barrier = pltpu.get_barrier_semaphore()
+
+    @pl.when(s > 0)
+    def _():
+        pl.semaphore_signal(barrier, inc=1, device_id=left, device_id_type=MESH)
+
+    @pl.when(s < seq - 1)
+    def _():
+        pl.semaphore_signal(barrier, inc=1, device_id=right, device_id_type=MESH)
+
+    pl.semaphore_wait(barrier, 2 - (seq - s) // seq - (s + 1) // seq)
+
+    up = pltpu.make_async_remote_copy(
+        src_ref=x.at[pl.ds(rows - width, width)],
+        dst_ref=before,
+        send_sem=send_sem.at[0],
+        recv_sem=recv_sem.at[0],
+        device_id=right,
+        device_id_type=MESH,
+    )
+    down = pltpu.make_async_remote_copy(
+        src_ref=x.at[pl.ds(0, width)],
+        dst_ref=after,
+        send_sem=send_sem.at[1],
+        recv_sem=recv_sem.at[1],
+        device_id=left,
+        device_id_type=MESH,
+    )
+
+    @pl.when(s < seq - 1)
+    def _():
+        up.start()
+
+    @pl.when(s > 0)
+    def _():
+        down.start()
+
+    @pl.when(s == 0)
+    def _():
+        before[...] = jnp.zeros_like(before)
+
+    @pl.when(s == seq - 1)
+    def _():
+        after[...] = jnp.zeros_like(after)
+
+    @pl.when(s > 0)
+    def _():
+        up.wait_recv()
+        down.wait_send()
+
+    @pl.when(s < seq - 1)
+    def _():
+        down.wait_recv()
+        up.wait_send()
+
+
+def with_halo(x, reach):
+    width = (reach + 15) // 16 * 16
+    side = jax.ShapeDtypeStruct((width, x.shape[1]), x.dtype)
+    before, after = pl.pallas_call(
+        functools.partial(halo_kernel, lax.axis_size("seq")),
+        out_shape=(side, side),
+        in_specs=[pl.BlockSpec(memory_space=pltpu.VMEM)],
+        out_specs=(pl.BlockSpec(memory_space=pltpu.VMEM),) * 2,
+        scratch_shapes=[pltpu.SemaphoreType.DMA((2,)), pltpu.SemaphoreType.DMA((2,))],
+        compiler_params=pltpu.CompilerParams(
+            collective_id=1, has_side_effects=True, vmem_limit_bytes=4 << 20
+        ),
+    )(x)
+    return jnp.concatenate([before[width - reach :], x, after[:reach]], axis=0)
 
 
 def layer_norm(values, gain):
@@ -365,7 +428,7 @@
         jnp.bfloat16
     )
     reach = depth_kernel.shape[0] // 2
-    padded = padded_2(gated, (("seq", 0),), reach)
+    padded = with_halo(gated, reach)
     depth = jnp.zeros((token_count, model_width), jnp.float32)
     for offset in range(depth_kernel.shape[0]):
         depth = (

time: 93.7 us -> 94.4 us (level)
  Pallas kernels: 72.6 us -> 77.4 us
  starting transfers between devices: 4.5 us -> 0 us
  local copies, waits for them, and re-layouts: 0.66 us -> 3.85 us
  waiting for transfers between devices: 3.03 us -> 0 us
    ppermute x2 -> x0, starting transfers between devices: 4.5 us -> none  [the longest x1 3.2 us: padded_2(): before = lax.ppermute(last, axis, up)]
    pallas_call x0 -> x1, Pallas kernels: none -> 3.97 us  [with_halo(): pl.pallas_call(functools.partial(halo_kernel, lax.axis_size('seq')), out_...]
    ppermute x2 -> x0, waiting for transfers between devices: 3.03 us -> none  [the longest x1 3.03 us: padded_2(): after = lax.ppermute(initial, axis, down)]
    slice x2, local copies, waits for them, and re-layouts: 0.1 us -> 2.54 us  [local(): depth_kernel[offset]]
  transfers between devices with their start and end apart: 2 -> 0, of which waited for: 1 -> 0; matrix products, arithmetic and copies ran while one was open for 0% -> 0% of each run, Pallas kernels for 0% -> 0%
where the time goes in v3:
time: 94.4 us; the launch traced here: 93.9 us
  Pallas kernels  77.4 us (82%)
  matrix products  8.1 us (9%)
  local copies, waits for them, and re-layouts  3.85 us (4%)
  other arithmetic  3.56 us (4%)
  between operations  1.03 us (1%)
    pallas_call x1, Pallas kernels, exchange(): pl.pallas_call(functools.partial(exchange_kernel, seq), out_shape=jax.Sha...  73.4 us
    pallas_call x1, Pallas kernels, with_halo(): pl.pallas_call(functools.partial(halo_kernel, lax.axis_size('seq')), out_...  3.97 us
    dot_general x1, matrix products, local(): lifted = jnp.dot(conv_in, point_in, preferred_element_type=jnp.float32)  3.11 us
    dot_general x1, matrix products, local(): jnp.dot(swished, point_out, preferred_element_type=jnp.float32)  2.76 us
    slice x2, local copies, waits for them, and re-layouts, local(): depth_kernel[offset]  2.54 us

profile of v3, /device:TPU:3, one launch (start us, length us, event | category | flops | bytes accessed | tf_op | source)
XLA Modules:
  0.0 93.9 jit_solution(13073929669420779888)
XLA Ops:
  0.0 0.0 copy-start
  0.8 1.1 %convert_reduce_fusion = f32[128]{0:T(128)S(1)} fusion(bf16[1,128,1024]{2,1,0:T(8,128)(2,1)} %param.14), kind=kLoop, calls=%fused_computation.38 | loop fusion | flops 262016 | bytes 262656 | tf_op jit(solution)/shard_map/reduce_sum | solution.py:88
  1.9 1.2 %fusion.8 = f32[128]{0:T(128)S(1)} fusion(bf16[1,128,1024]{2,1,0:T(8,128)(2,1)} %param.14, f32[128]{0:T(128)S(1)} %broadcast_multiply_fusion.1), kind=kLoop, calls=%fused_computation.43 | loop fusion | flops 524160 | bytes 263168 | tf_op jit(solution)/shard_map/reduce_sum | solution.py:89
  3.1 0.8 slice_bitcast_fusion.1
  3.8 0.2 select_reduce_fusion.1
  4.0 0.8 fusion.68
  4.8 1.1 %fusion.72 = (f32[1,1024]{1,0:T(1,128)S(1)}, f32[1,1024]{1,0:T(1,128)S(1)}, f32[1,1024]{1,0:T(1,128)S(1)}, f32[1,1024]{1,0:T(1,128)S(1)}, f32[1,1024]{1,0:T(1,12...) fusion(f32[31,1024]{1,0:T(8,128)} %param.19), kind=kLoop, calls=%fused_computation.150 | loop fusion | bytes 98304 | tf_op jit(solution)/shard_map/slice | solution.py:435
  5.9 1.4 %fusion.71 = (f32[1,1024]{1,0:T(1,128)S(1)}, f32[1,1024]{1,0:T(1,128)S(1)}, f32[1,1024]{1,0:T(1,128)S(1)}, f32[1,1024]{1,0:T(1,128)S(1)}, f32[1,1024]{1,0:T(1,12...) fusion(f32[31,1024]{1,0:T(8,128)} %param.19), kind=kLoop, calls=%fused_computation.149 | loop fusion | bytes 155648 | tf_op jit(solution)/shard_map/slice | solution.py:435
  7.3 0.0 copy-start.4
  7.3 0.0 copy-start.7
  7.3 0.0 copy-start.8
  7.4 3.1 %fusion.17 = f32[128,2048]{1,0:T(8,128)S(1)} fusion(bf16[1024,2048]{1,0:T(8,128)(2,1)} %param.18, bf16[1,128,1024]{2,1,0:T(8,128)(2,1)} %param.14, f32[1024]{0:T(1024)} %param.17, f32[128]{0:T(128)S(1)} %add_rsqrt_fusion.1, f32[128]{0:T(128)S(1)} %broadcast_multiply_fusion.1), kind=kOutput, calls=%fused_computation.56 | convolution fusion | flops 537526272 | bytes 5510144 | tf_op jit(solution)/shard_map/dot_general | solution.py:426
  10.5 0.2 fusion.16.x
  10.6 4.0 %shard_map.136 = (bf16[16,1024]{1,0:T(8,128)(2,1)S(1)}, bf16[16,1024]{1,0:T(8,128)(2,1)S(1)}) custom-call(bf16[128,1024]{1,0:T(8,128)(2,1)S(1)} %fusion.16.x), custom_call_target="tpu_custom_call" | custom-call | tf_op jit(solution)/shard_map/pallas_call | solution.py:73
  14.6 0.0 copy-done
  14.6 0.0 copy-done.4
  14.7 0.0 copy-done.7
  14.7 0.0 copy-start.6
  14.7 0.0 copy-start.5
  14.7 0.0 copy-start.2
  14.7 0.0 copy-start.3
  14.7 2.8 %fusion.73 = (f32[128]{0:T(128)S(1)}, f32[128,1024]{1,0:T(8,128)S(1)}) fusion(bf16[1024,1024]{1,0:T(8,128)(2,1)S(1)} %copy-done, bf16[128,1024]{1,0:T(8,128)(2,1)S(1)} %fusion.16.x, bf16[15,1024]{1,0:T(8,128)(2,1)S(1)} %bitcast.88, bf16[15,1024]{1,0:T(8,128)(2,1)S(1)} %slice.235, f32[1024]{0:T(1024)S(1)} %copy-done.7, f32[1024]{0:T(1024)S(1)} %copy-done.8, ...), kind=kOutput, calls=%fused_computation.151 | convolution fusion | flops 293601152 | bytes 3342848 | tf_op jit(solution)/shard_map/dot_general | solution.py:438
  17.5 0.2 multiply_reduce_fusion
  17.7 0.1 multiply_convert_fusion
  17.9 0.2 fusion.62
  18.1 0.5 convolution_convert_fusion
  18.6 0.0 copy-done.2
  18.6 0.0 copy-done.3
  18.6 0.5 copy-done.1
  19.1 73.4 %shard_map.137 = bf16[8,48,1024]{2,1,0:T(8,128)(2,1)S(1)} custom-call(bf16[8,48,1024]{2,1,0:T(8,128)(2,1)S(1)} %bitcast.84, bf16[1024,1024]{1,0:T(8,128)(2,1)S(1)} %bitcast.85, bf16[1024,1024]{1,0:T(8,128)(2,1)S(1)} %bitcast.86, bf16[1024,1024]{1,0:T(8,128)(2,1)S(1)} %bitcast.87), custom_call_target="tpu_custom_call" | custom-call | flops 9663676416 | bytes 6291456 | tf_op jit(solution)/shard_map/pallas_call | solution.py:345
  92.5 0.4 fusion.2
  92.8 1.1 %fusion.4 = bf16[1,128,1024]{2,1,0:T(8,128)(2,1)} fusion(f32[128,1024]{1,0:T(8,128)S(1)} %fusion.2, bf16[384,1024]{1,0:T(8,128)(2,1)S(1)} %bitcast.83, f32[128]{0:T(128)S(1)} %get-tuple-element.44, f32[128]{0:T(128)S(1)} %compare_convert_fusion, s32[128]{0:T(128)S(1)} %get-tuple-element.47), kind=kOutput, calls=%fused_computation.36 | convolution fusion | flops 101236736 | bytes 1574400 | tf_op jit(solution)/shard_map/dot_general | solution.py:478
  (11 shorter events, 0.1 us)
Async XLA Ops:
  0.0 14.6 %copy-start = (bf16[1024,1024]{1,0:T(8,128)(2,1)S(1)}, bf16[1024,1024]{1,0:T(8,128)(2,1)}, u32[]{:S(2)}) copy-start(bf16[1024,1024]{1,0:T(8,128)(2,1)} %param.22) | copy-start | bytes 6291460
  7.3 7.3 %copy-start.4 = (bf16[1,128,1024]{2,1,0:T(8,128)(2,1)S(1)}, bf16[1,128,1024]{2,1,0:T(8,128)(2,1)}, u32[]{:S(2)}) copy-start(bf16[1,128,1024]{2,1,0:T(8,128)(2,1)} %param.14) | copy-start | bytes 786436
  7.3 7.3 %copy-start.7 = (f32[1024]{0:T(1024)S(1)}, f32[1024]{0:T(1024)}, u32[]{:S(2)}) copy-start(f32[1024]{0:T(1024)} %param.21) | copy-start | bytes 12292
  7.3 7.3 %copy-start.8 = (f32[1024]{0:T(1024)S(1)}, f32[1024]{0:T(1024)}, u32[]{:S(2)}) copy-start(f32[1024]{0:T(1024)} %param.20) | copy-start | bytes 12292
  14.7 3.0 %copy-start.6 = (f32[1024]{0:T(1024)S(1)}, f32[1024]{0:T(1024)}, u32[]{:S(2)}) copy-start(f32[1024]{0:T(1024)} %param.23) | copy-start | bytes 12292
  14.7 3.2 %copy-start.5 = (bf16[1024,8]{0,1:T(8,128)(2,1)S(1)}, bf16[1024,8]{0,1:T(8,128)(2,1)}, u32[]{:S(2)}) copy-start(bf16[1024,8]{0,1:T(8,128)(2,1)} %param.24) | copy-start | bytes 49156
  14.7 3.9 %copy-start.2 = (bf16[1,1024,1024]{2,1,0:T(8,128)(2,1)S(1)}, bf16[1,1024,1024]{2,1,0:T(8,128)(2,1)}, u32[]{:S(2)}) copy-start(bf16[1,1024,1024]{2,1,0:T(8,128)(2,1)} %param.26) | copy-start | bytes 6291460
  14.7 3.9 %copy-start.3 = (bf16[1,1024,1024]{2,1,0:T(8,128)(2,1)S(1)}, bf16[1,1024,1024]{2,1,0:T(8,128)(2,1)}, u32[]{:S(2)}) copy-start(bf16[1,1024,1024]{2,1,0:T(8,128)(2,1)} %param.27) | copy-start | bytes 6291460
  17.5 1.6 %copy-start.1 = (bf16[1,1024,1024]{2,1,0:T(8,128)(2,1)S(1)}, bf16[1,1024,1024]{2,1,0:T(8,128)(2,1)}, u32[]{:S(2)}) copy-start(bf16[1,1024,1024]{2,1,0:T(8,128)(2,1)} %param.25) | copy-start | bytes 6291460

commit v4 on v3

--- a/solution.py
+++ b/solution.py
@@ -7,7 +7,7 @@
 from jax.sharding import PartitionSpec as P
 
 
-def halo_kernel(seq, x, before, after, send_sem, recv_sem):
+def halo_kernel(seq, x, taps, scale, shift, out, before, after, padded, send_sem, recv_sem):
     d, s, c = lax.axis_index("dp"), lax.axis_index("seq"), lax.axis_index("expert")
     width, rows = before.shape[0], x.shape[0]
     left, right = (d, (s + seq - 1) % seq, c), (d, (s + 1) % seq, c)
@@ -56,6 +56,8 @@
     def _():
         after[...] = jnp.zeros_like(after)
 
+    padded[pl.ds(width, rows), :] = x[...].astype(jnp.float32)
+
     @pl.when(s > 0)
     def _():
         up.wait_recv()
@@ -66,21 +68,40 @@
         down.wait_recv()
         up.wait_send()
 
-
-def with_halo(x, reach):
-    width = (reach + 15) // 16 * 16
-    side = jax.ShapeDtypeStruct((width, x.shape[1]), x.dtype)
-    before, after = pl.pallas_call(
+    padded[pl.ds(0, width), :] = before[...].astype(jnp.float32)
+    padded[pl.ds(width + rows, width), :] = after[...].astype(jnp.float32)
+    reach = taps.shape[0] // 2
+
+    @pl.loop(0, x.shape[1] // 128)
+    def _(n):
+        columns = pl.ds(pl.multiple_of(n * 128, 128), 128)
+        depth = jnp.zeros((rows, 128), jnp.float32)
+        for t in range(taps.shape[0]):
+            depth += padded[pl.ds(width - reach + t, rows), columns] * taps[pl.ds(t, 1), columns]
+        v = depth * scale[:, columns] + shift[:, columns]
+        out[:, columns] = (v / (1.0 + jnp.exp(-v))).astype(jnp.bfloat16)
+
+
+def depthwise(x, taps, scale, shift):
+    rows, features = x.shape
+    width = (taps.shape[0] // 2 + 15) // 16 * 16
+    dma = pltpu.SemaphoreType.DMA
+    return pl.pallas_call(
         functools.partial(halo_kernel, lax.axis_size("seq")),
-        out_shape=(side, side),
-        in_specs=[pl.BlockSpec(memory_space=pltpu.VMEM)],
-        out_specs=(pl.BlockSpec(memory_space=pltpu.VMEM),) * 2,
-        scratch_shapes=[pltpu.SemaphoreType.DMA((2,)), pltpu.SemaphoreType.DMA((2,))],
+        out_shape=jax.ShapeDtypeStruct(x.shape, x.dtype),
+        in_specs=[pl.BlockSpec(memory_space=pltpu.VMEM)] * 4,
+        out_specs=pl.BlockSpec(memory_space=pltpu.VMEM),
+        scratch_shapes=[
+            pltpu.VMEM((width, features), x.dtype),
+            pltpu.VMEM((width, features), x.dtype),
+            pltpu.VMEM((rows + 2 * width, features), jnp.float32),
+            dma((2,)),
+            dma((2,)),
+        ],
         compiler_params=pltpu.CompilerParams(
-            collective_id=1, has_side_effects=True, vmem_limit_bytes=4 << 20
+            collective_id=1, has_side_effects=True, vmem_limit_bytes=8 << 20
         ),
-    )(x)
-    return jnp.concatenate([before[width - reach :], x, after[:reach]], axis=0)
+    )(x, taps, scale[None, :], shift[None, :])
 
 
 def layer_norm(values, gain):
@@ -427,14 +448,7 @@
     gated = (lifted[:, :model_width] * jax.nn.sigmoid(lifted[:, model_width:]) * frame_mask).astype(
         jnp.bfloat16
     )
-    reach = depth_kernel.shape[0] // 2
-    padded = with_halo(gated, reach)
-    depth = jnp.zeros((token_count, model_width), jnp.float32)
-    for offset in range(depth_kernel.shape[0]):
-        depth = (
-            depth + padded[offset : offset + token_count].astype(jnp.float32) * depth_kernel[offset]
-        )
-    swished = jax.nn.silu(depth * bn_scale + bn_shift).astype(jnp.bfloat16)
+    swished = depthwise(gated, depth_kernel, bn_scale, bn_shift)
     residual = frame_rows.astype(jnp.float32) + jnp.dot(
         swished, point_out, preferred_element_type=jnp.float32
     )

time: 94.4 us -> 92.7 us (0.982)
  Pallas kernels: 77.4 us -> 80.5 us
  local copies, waits for them, and re-layouts: 3.85 us -> 1.52 us
  matrix products: 8.1 us -> 5.86 us
    pallas_call x1, Pallas kernels: 3.97 us -> 7.08 us  [depthwise(): pl.pallas_call(functools.partial(halo_kernel, lax.axis_size('seq')), out_...]
    slice x3 -> x0, local copies, waits for them, and re-layouts: 2.55 us -> none  [the longest x2 2.54 us: local(): depth_kernel[offset]]
    dot_general x1, matrix products: 2.76 us -> 0.53 us  [local(): jnp.dot(swished, point_out, preferred_element_type=jnp.float32)]
where the time goes in v4:
time: 92.7 us; the launch traced here: 92.4 us
  Pallas kernels  80.5 us (87%)
  matrix products  5.86 us (6%)
  other arithmetic  3.56 us (4%)
  local copies, waits for them, and re-layouts  1.52 us (2%)
  between operations  1.01 us (1%)
    pallas_call x1, Pallas kernels, exchange(): pl.pallas_call(functools.partial(exchange_kernel, seq), out_shape=jax.Sha...  73.4 us
    pallas_call x1, Pallas kernels, depthwise(): pl.pallas_call(functools.partial(halo_kernel, lax.axis_size('seq')), out_...  7.08 us
    dot_general x1, matrix products, local(): lifted = jnp.dot(conv_in, point_in, preferred_element_type=jnp.float32)  3.11 us

profile of v4, /device:TPU:3, one launch (start us, length us, event | category | flops | bytes accessed | tf_op | source)
XLA Modules:
  0.0 92.4 jit_solution(12191406208534118089)
XLA Ops:
  0.0 0.0 copy-start
  0.8 1.1 %convert_reduce_fusion = f32[128]{0:T(128)S(1)} fusion(bf16[1,128,1024]{2,1,0:T(8,128)(2,1)} %param.14), kind=kLoop, calls=%fused_computation.10 | loop fusion | flops 262016 | bytes 262656 | tf_op jit(solution)/shard_map/reduce_sum | solution.py:109
  1.9 1.2 %fusion.8 = f32[128]{0:T(128)S(1)} fusion(bf16[1,128,1024]{2,1,0:T(8,128)(2,1)} %param.14, f32[128]{0:T(128)S(1)} %broadcast_multiply_fusion.1), kind=kLoop, calls=%fused_computation.15 | loop fusion | flops 524160 | bytes 263168 | tf_op jit(solution)/shard_map/reduce_sum | solution.py:110
  3.1 0.8 slice_bitcast_fusion.1
  3.8 0.2 select_reduce_fusion.1
  4.0 0.8 fusion.40
  4.8 3.1 %fusion.17 = f32[128,2048]{1,0:T(8,128)S(1)} fusion(bf16[1024,2048]{1,0:T(8,128)(2,1)} %param.18, bf16[1,128,1024]{2,1,0:T(8,128)(2,1)} %param.14, f32[1024]{0:T(1024)} %param.17, f32[128]{0:T(128)S(1)} %add_rsqrt_fusion.1, f32[128]{0:T(128)S(1)} %broadcast_multiply_fusion.1), kind=kOutput, calls=%fused_computation.27 | convolution fusion | flops 537526272 | bytes 5510144 | tf_op jit(solution)/shard_map/dot_general | solution.py:447
  7.9 0.0 copy-start.7
  7.9 0.2 fusion.16.x
  8.1 0.0 copy-done.1
  8.1 0.0 copy-done.2
  8.1 0.0 copy-done.3
  8.1 0.0 copy-start.9
  8.1 0.0 copy-start.6
  8.1 7.1 %shard_map.136 = bf16[128,1024]{1,0:T(8,128)(2,1)S(1)} custom-call(bf16[128,1024]{1,0:T(8,128)(2,1)S(1)} %fusion.16.x, f32[31,1024]{1,0:T(8,128)S(1)} %copy-done.1, f32[1,1024]{1,0:T(1,128)S(1)} %bitcast.56, f32[1,1024]{1,0:T(1,128)S(1)} %bitcast.57), custom_call_target="tpu_custom_call" | custom-call | tf_op jit(solution)/shard_map/pallas_call | solution.py:89
  15.2 0.0 copy-done
  15.2 0.0 copy-done.7
  15.2 0.0 copy-start.8
  15.2 0.0 copy-start.5
  15.3 0.5 fusion.41
  15.8 0.0 copy-start.4
  15.8 0.2 multiply_reduce_fusion
  16.0 0.0 copy-done.9
  16.0 0.1 multiply_convert_fusion
  16.2 0.0 copy-done.8
  16.2 0.2 fusion.34
  16.4 0.5 convolution_convert_fusion
  16.9 0.0 copy-done.6
  16.9 0.7 copy-done.4
  17.6 73.4 %shard_map.137 = bf16[8,48,1024]{2,1,0:T(8,128)(2,1)S(1)} custom-call(bf16[8,48,1024]{2,1,0:T(8,128)(2,1)S(1)} %bitcast.55, bf16[1024,1024]{1,0:T(8,128)(2,1)S(1)} %bitcast.58, bf16[1024,1024]{1,0:T(8,128)(2,1)S(1)} %bitcast.59, bf16[1024,1024]{1,0:T(8,128)(2,1)S(1)} %bitcast.60), custom_call_target="tpu_custom_call" | custom-call | flops 9663676416 | bytes 6291456 | tf_op jit(solution)/shard_map/pallas_call | solution.py:366
  91.0 0.4 fusion.2
  91.4 1.1 %fusion.4 = bf16[1,128,1024]{2,1,0:T(8,128)(2,1)} fusion(f32[128,1024]{1,0:T(8,128)S(1)} %fusion.2, bf16[384,1024]{1,0:T(8,128)(2,1)S(1)} %bitcast.54, f32[128]{0:T(128)S(1)} %get-tuple-element.9, f32[128]{0:T(128)S(1)} %compare_convert_fusion, s32[128]{0:T(128)S(1)} %get-tuple-element.12), kind=kOutput, calls=%fused_computation.8 | convolution fusion | flops 101236736 | bytes 1574400 | tf_op jit(solution)/shard_map/dot_general | solution.py:492
  (10 shorter events, 0.1 us)
Async XLA Ops:
  0.0 15.2 %copy-start = (bf16[1024,1024]{1,0:T(8,128)(2,1)S(1)}, bf16[1024,1024]{1,0:T(8,128)(2,1)}, u32[]{:S(2)}) copy-start(bf16[1024,1024]{1,0:T(8,128)(2,1)} %param.22) | copy-start | bytes 6291460
  4.8 3.3 %copy-start.1 = (f32[31,1024]{1,0:T(8,128)S(1)}, f32[31,1024]{1,0:T(8,128)}, u32[]{:S(2)}) copy-start(f32[31,1024]{1,0:T(8,128)} %taps.1) | copy-start | bytes 380932
  4.8 3.3 %copy-start.2 = (f32[1024]{0:T(1024)S(1)}, f32[1024]{0:T(1024)}, u32[]{:S(2)}) copy-start(f32[1024]{0:T(1024)} %param.20) | copy-start | bytes 12292
  4.8 3.3 %copy-start.3 = (f32[1024]{0:T(1024)S(1)}, f32[1024]{0:T(1024)}, u32[]{:S(2)}) copy-start(f32[1024]{0:T(1024)} %param.21) | copy-start | bytes 12292
  7.9 7.3 %copy-start.7 = (bf16[1,128,1024]{2,1,0:T(8,128)(2,1)S(1)}, bf16[1,128,1024]{2,1,0:T(8,128)(2,1)}, u32[]{:S(2)}) copy-start(bf16[1,128,1024]{2,1,0:T(8,128)(2,1)} %param.14) | copy-start | bytes 786436
  8.1 7.9 %copy-start.9 = (f32[1024]{0:T(1024)S(1)}, f32[1024]{0:T(1024)}, u32[]{:S(2)}) copy-start(f32[1024]{0:T(1024)} %param.23) | copy-start | bytes 12292
  8.1 8.8 %copy-start.6 = (bf16[1,1024,1024]{2,1,0:T(8,128)(2,1)S(1)}, bf16[1,1024,1024]{2,1,0:T(8,128)(2,1)}, u32[]{:S(2)}) copy-start(bf16[1,1024,1024]{2,1,0:T(8,128)(2,1)} %param.27) | copy-start | bytes 6291460
  15.2 0.9 %copy-start.8 = (bf16[1024,8]{0,1:T(8,128)(2,1)S(1)}, bf16[1024,8]{0,1:T(8,128)(2,1)}, u32[]{:S(2)}) copy-start(bf16[1024,8]{0,1:T(8,128)(2,1)} %param.24) | copy-start | bytes 49156
  15.2 1.6 %copy-start.5 = (bf16[1,1024,1024]{2,1,0:T(8,128)(2,1)S(1)}, bf16[1,1024,1024]{2,1,0:T(8,128)(2,1)}, u32[]{:S(2)}) copy-start(bf16[1,1024,1024]{2,1,0:T(8,128)(2,1)} %param.26) | copy-start | bytes 6291460
  15.8 1.8 %copy-start.4 = (bf16[1,1024,1024]{2,1,0:T(8,128)(2,1)S(1)}, bf16[1,1024,1024]{2,1,0:T(8,128)(2,1)}, u32[]{:S(2)}) copy-start(bf16[1,1024,1024]{2,1,0:T(8,128)(2,1)} %param.25) | copy-start | bytes 6291460
